TPU v7x, 128 devices: a whole 4x4x4 slice. The times are simulated.
128 devices in a mesh: rep: 2 (over y_lo), fsdp: 8 (over z, y_hi), tp: 8 (over x, core).
Axes of the slice: x: 4, y: 4 (y_hi: 2, y_lo: 2; y = y_hi * 2 + y_lo), z: 4, core: 2. Of those that a mesh axis runs over, the one named last changes fastest.
Arguments:
- images: bfloat16 [16, 577, 1024], P(('rep', 'fsdp')), may hold values from -6 to 6
- cotangent: bfloat16 [16, 577, 1024], P(('rep', 'fsdp')), may hold values from -6 to 6
- norm1_gain: float32 [2, 1024], replicated, may hold values from 0.1 to 1.9
- norm1_shift: float32 [2, 1024], replicated, may hold values from -3 to 3
- qkv_weight: bfloat16 [2, 1024, 3, 1024], P(None, 'fsdp', None, 'tp'), may hold values from -0.1875 to 0.1875
- qv_bias: float32 [2, 2, 1024], P(None, None, 'tp'), may hold values from -3 to 3
- out_weight: bfloat16 [2, 1024, 1024], P(None, 'tp', 'fsdp'), may hold values from -0.75 to 0.75
- out_bias: float32 [2, 1024], replicated, may hold values from -3 to 3
- norm2_gain: float32 [2, 1024], replicated, may hold values from 0.1 to 1.9
- norm2_shift: float32 [2, 1024], replicated, may hold values from -3 to 3
- up_weight: bfloat16 [2, 1024, 4096], P(None, 'fsdp', 'tp'), may hold values from -0.1875 to 0.1875
- up_bias: float32 [2, 4096], P(None, 'tp'), may hold values from -3 to 3
- down_weight: bfloat16 [2, 4096, 1024], P(None, 'tp', 'fsdp'), may hold values from -0.09375 to 0.09375
- down_bias: float32 [2, 1024], replicated, may hold values from -5 to 5
Outputs:
- out_act: float32 [16, 577, 1024], P(('rep', 'fsdp'))
- grad_images: float32 [16, 577, 1024], P(('rep', 'fsdp'))
- grad_norm1_gain: float32 [2, 1024], replicated
- grad_norm1_shift: float32 [2, 1024], replicated
- grad_qkv_weight: float32 [2, 1024, 3, 1024], P(None, 'fsdp', None, 'tp')
- grad_qv_bias: float32 [2, 2, 1024], P(None, None, 'tp')
- grad_out_weight: float32 [2, 1024, 1024], P(None, 'tp', 'fsdp')
- grad_out_bias: float32 [2, 1024], replicated
- grad_norm2_gain: float32 [2, 1024], replicated
- grad_norm2_shift: float32 [2, 1024], replicated
- grad_up_weight: float32 [2, 1024, 4096], P(None, 'fsdp', 'tp')
- grad_up_bias: float32 [2, 4096], P(None, 'tp')
- grad_down_weight: float32 [2, 4096, 1024], P(None, 'tp', 'fsdp')
- grad_down_bias: float32 [2, 1024], replicated
All inputs are finite; a program needn't handle non-finite values.
Results may differ from a plain program's by a relative error of at most 0.012.
Values may be sent and summed in bfloat16 or wider, within the bound.
No kernel may reach another device: no remote copies, remote signals or barrier semaphores. Data moves between devices by JAX's collectives and lax.ppermute only.
A program may use at most 128 MiB of HBM per device.

v0:
```python
import jax
import jax.numpy as jnp
from jax import lax
from jax.sharding import PartitionSpec as P

HEAD_DIM = 64
EPSILON = 1e-05


def norm_forward(values_in, norm_gain, norm_shift):
    row_mean = jnp.mean(values_in, -1, keepdims=True)
    centred = values_in - row_mean
    inv_std = lax.rsqrt(jnp.mean(centred * centred, -1, keepdims=True) + EPSILON)
    normed = centred * inv_std
    return (normed * norm_gain + norm_shift, normed, inv_std)


def norm_backward(upstream, normed, inv_std, norm_gain):
    scaled = upstream * norm_gain
    return inv_std * (
        scaled
        - jnp.mean(scaled, -1, keepdims=True)
        - normed * jnp.mean(scaled * normed, -1, keepdims=True)
    )


def gelu_parts(pre_act):
    normal_cdf = 0.5 * (1.0 + lax.erf(pre_act * 0.7071067811865476))
    normal_pdf = jnp.exp(-0.5 * pre_act * pre_act) * 0.3989422804014327
    return (pre_act * normal_cdf, normal_cdf + pre_act * normal_pdf)


def attend(queries, key_vecs, val_vecs):
    softmax_scale = HEAD_DIM ** (-0.5)
    scores = (
        jnp.einsum("bqhe,bkhe->bhqk", queries, key_vecs, preferred_element_type=jnp.float32)
        * softmax_scale
    )
    row_max = jnp.max(scores, -1, keepdims=True)
    log_total = row_max + jnp.log(jnp.sum(jnp.exp(scores - row_max), -1, keepdims=True))
    prob_b = jnp.exp(scores - log_total).astype(jnp.bfloat16)
    mixed_b = jnp.einsum(
        "bhqk,bkhe->bqhe", prob_b, val_vecs, preferred_element_type=jnp.float32
    ).astype(jnp.bfloat16)
    return (mixed_b, log_total)


def attend_back(queries, key_vecs, val_vecs, log_total, d_mixed):
    softmax_scale = HEAD_DIM ** (-0.5)
    scores = (
        jnp.einsum("bqhe,bkhe->bhqk", queries, key_vecs, preferred_element_type=jnp.float32)
        * softmax_scale
    )
    probs = jnp.exp(scores - log_total)
    prob_b = probs.astype(jnp.bfloat16)
    d_values = jnp.einsum("bhqk,bqhe->bkhe", prob_b, d_mixed, preferred_element_type=jnp.float32)
    d_probs = jnp.einsum("bqhe,bkhe->bhqk", d_mixed, val_vecs, preferred_element_type=jnp.float32)
    row_dot = jnp.sum(probs * d_probs, -1, keepdims=True)
    d_scores = (probs * (d_probs - row_dot) * softmax_scale).astype(jnp.bfloat16)
    d_queries = jnp.einsum(
        "bhqk,bkhe->bqhe", d_scores, key_vecs, preferred_element_type=jnp.float32
    )
    d_keys = jnp.einsum("bhqk,bqhe->bkhe", d_scores, queries, preferred_element_type=jnp.float32)
    return (d_queries, d_keys, d_values)


def branch_total(contrib):
    return lax.psum(contrib, "tp")


def input_total(contrib):
    return lax.psum(contrib, "tp")


def body(
    images,
    cotangent,
    norm1_gain,
    norm1_shift,
    qkv_weight,
    qv_bias,
    out_weight,
    out_bias,
    norm2_gain,
    norm2_shift,
    up_weight,
    up_bias,
    down_weight,
    down_bias,
):
    images_here, seq_len, model_width = images.shape
    row_count = images_here * seq_len
    layer_count = qkv_weight.shape[0]
    local_cols = qkv_weight.shape[3]
    heads_here = local_cols // HEAD_DIM
    head_shape = (images_here, seq_len, heads_here, HEAD_DIM)
    state = images.astype(jnp.float32).reshape(row_count, model_width)
    gradient = cotangent.astype(jnp.float32).reshape(row_count, model_width)
    saved = []
    for layer_idx in range(layer_count):
        qkv_full, out_full, up_full, down_full = (
            lax.all_gather(qkv_weight[layer_idx], "fsdp", axis=0, tiled=True),
            lax.all_gather(out_weight[layer_idx], "fsdp", axis=1, tiled=True),
            lax.all_gather(up_weight[layer_idx], "fsdp", axis=0, tiled=True),
            lax.all_gather(down_weight[layer_idx], "fsdp", axis=1, tiled=True),
        )
        normed_a, unit_a, inv_a = norm_forward(state, norm1_gain[layer_idx], norm1_shift[layer_idx])
        first_b = normed_a.astype(jnp.bfloat16)
        projected = jnp.einsum("rd,dtc->rtc", first_b, qkv_full, preferred_element_type=jnp.float32)
        queries = (projected[:, 0] + qv_bias[layer_idx, 0]).astype(jnp.bfloat16).reshape(head_shape)
        key_vecs = projected[:, 1].astype(jnp.bfloat16).reshape(head_shape)
        val_vecs = (
            (projected[:, 2] + qv_bias[layer_idx, 1]).astype(jnp.bfloat16).reshape(head_shape)
        )
        mixed_b, log_total = attend(queries, key_vecs, val_vecs)
        mixed_flat = mixed_b.reshape(row_count, local_cols)
        middle = (
            state
            + branch_total(jnp.dot(mixed_flat, out_full, preferred_element_type=jnp.float32))
            + out_bias[layer_idx]
        )
        normed_b, unit_b, inv_b = norm_forward(
            middle, norm2_gain[layer_idx], norm2_shift[layer_idx]
        )
        second_b = normed_b.astype(jnp.bfloat16)
        hidden = jnp.dot(second_b, up_full, preferred_element_type=jnp.float32) + up_bias[layer_idx]
        active, slopes = gelu_parts(hidden)
        active_b = active.astype(jnp.bfloat16)
        state = (
            middle
            + branch_total(jnp.dot(active_b, down_full, preferred_element_type=jnp.float32))
            + down_bias[layer_idx]
        )
        stored = ()
        saved.append(
            (
                stored,
                unit_a,
                inv_a,
                first_b,
                queries,
                key_vecs,
                val_vecs,
                log_total,
                mixed_flat,
                unit_b,
                inv_b,
                second_b,
                slopes,
                active_b,
            )
        )
    owned_grads = [None] * layer_count
    small_grads = [None] * layer_count
    for layer_idx in reversed(range(layer_count)):
        (
            stored,
            unit_a,
            inv_a,
            first_b,
            queries,
            key_vecs,
            val_vecs,
            log_total,
            mixed_flat,
            unit_b,
            inv_b,
            second_b,
            slopes,
            active_b,
        ) = saved[layer_idx]
        qkv_full, out_full, up_full, down_full = (
            lax.all_gather(qkv_weight[layer_idx], "fsdp", axis=0, tiled=True),
            lax.all_gather(out_weight[layer_idx], "fsdp", axis=1, tiled=True),
            lax.all_gather(up_weight[layer_idx], "fsdp", axis=0, tiled=True),
            lax.all_gather(down_weight[layer_idx], "fsdp", axis=1, tiled=True),
        )
        d_down_bias = jnp.sum(gradient, 0)
        grad_b = gradient.astype(jnp.bfloat16)
        d_down = jnp.einsum("rf,rd->fd", active_b, grad_b, preferred_element_type=jnp.float32)
        d_hidden = (
            jnp.einsum("rd,fd->rf", grad_b, down_full, preferred_element_type=jnp.float32) * slopes
        )
        d_up_bias = jnp.sum(d_hidden, 0)
        d_hidden_b = d_hidden.astype(jnp.bfloat16)
        d_up = jnp.einsum("rd,rf->df", second_b, d_hidden_b, preferred_element_type=jnp.float32)
        d_norm_two = input_total(
            jnp.einsum("rf,df->rd", d_hidden_b, up_full, preferred_element_type=jnp.float32)
        )
        d_gain_two = jnp.sum(d_norm_two * unit_b, 0)
        d_shift_two = jnp.sum(d_norm_two, 0)
        grad_mid = gradient + norm_backward(d_norm_two, unit_b, inv_b, norm2_gain[layer_idx])
        d_out_bias = jnp.sum(grad_mid, 0)
        mid_b = grad_mid.astype(jnp.bfloat16)
        d_out = jnp.einsum("rc,rd->cd", mixed_flat, mid_b, preferred_element_type=jnp.float32)
        d_mixed = (
            jnp.einsum("rd,cd->rc", mid_b, out_full, preferred_element_type=jnp.float32)
            .astype(jnp.bfloat16)
            .reshape(head_shape)
        )
        d_queries, d_keys, d_values = attend_back(queries, key_vecs, val_vecs, log_total, d_mixed)
        d_queries = d_queries.reshape(row_count, local_cols)
        d_keys = d_keys.reshape(row_count, local_cols)
        d_values = d_values.reshape(row_count, local_cols)
        d_qv_bias = jnp.stack([jnp.sum(d_queries, 0), jnp.sum(d_values, 0)])
        d_proj_b = jnp.stack([d_queries, d_keys, d_values], 1).astype(jnp.bfloat16)
        d_qkv = jnp.einsum("rd,rtc->dtc", first_b, d_proj_b, preferred_element_type=jnp.float32)
        d_norm_one = input_total(
            jnp.einsum("rtc,dtc->rd", d_proj_b, qkv_full, preferred_element_type=jnp.float32)
        )
        d_gain_one = jnp.sum(d_norm_one * unit_a, 0)
        d_shift_one = jnp.sum(d_norm_one, 0)
        gradient = grad_mid + norm_backward(d_norm_one, unit_a, inv_a, norm1_gain[layer_idx])
        small_grads[layer_idx] = (
            d_gain_one,
            d_shift_one,
            d_qv_bias,
            d_out_bias,
            d_gain_two,
            d_shift_two,
            d_up_bias,
            d_down_bias,
        )
        shares = (
            lax.psum_scatter(d_qkv, "fsdp", scatter_dimension=0, tiled=True),
            lax.psum_scatter(d_out, "fsdp", scatter_dimension=1, tiled=True),
            lax.psum_scatter(d_up, "fsdp", scatter_dimension=0, tiled=True),
            lax.psum_scatter(d_down, "fsdp", scatter_dimension=1, tiled=True),
        )
        owned_grads[layer_idx] = lax.psum((shares[0], shares[1], shares[2], shares[3]), "rep")
    big_grads = tuple(
        (
            jnp.stack([owned_grads[layer_idx][member] for layer_idx in range(layer_count)])
            for member in range(4)
        )
    )
    small_stack = [
        jnp.stack([small_grads[layer_idx][member] for layer_idx in range(layer_count)])
        for member in range(8)
    ]
    reduced = lax.psum(
        (
            small_stack[0],
            small_stack[1],
            small_stack[2],
            small_stack[3],
            small_stack[4],
            small_stack[5],
            small_stack[6],
            small_stack[7],
        ),
        ("rep", "fsdp"),
    )
    output = state.reshape(images_here, seq_len, model_width)
    grad_images = gradient.reshape(images_here, seq_len, model_width)
    return (
        output,
        grad_images,
        reduced[0],
        reduced[1],
        big_grads[0],
        reduced[2],
        big_grads[1],
        reduced[3],
        reduced[4],
        reduced[5],
        big_grads[2],
        reduced[6],
        big_grads[3],
        reduced[7],
    )


def solution(mesh):
    in_specs = (
        P(("rep", "fsdp"), None, None),
        P(("rep", "fsdp"), None, None),
        P(),
        P(),
        P(None, "fsdp", None, "tp"),
        P(None, None, "tp"),
        P(None, "tp", "fsdp"),
        P(),
        P(),
        P(),
        P(None, "fsdp", "tp"),
        P(None, "tp"),
        P(None, "tp", "fsdp"),
        P(),
    )
    out_specs = (
        P(("rep", "fsdp"), None, None),
        P(("rep", "fsdp"), None, None),
        P(),
        P(),
        P(None, "fsdp", None, "tp"),
        P(None, None, "tp"),
        P(None, "tp", "fsdp"),
        P(),
        P(),
        P(),
        P(None, "fsdp", "tp"),
        P(None, "tp"),
        P(None, "tp", "fsdp"),
        P(),
    )
    return jax.shard_map(body, mesh=mesh, in_specs=in_specs, out_specs=out_specs, check_vma=False)
```

profile of v0, /device:TPU:0, one launch (start us, length us, event | category | flops | bytes accessed | tf_op | source)
XLA Modules:
  0.0 1286.5 jit_solution(16832507435293279262)
XLA Ops:
  9.7 1.7 fusion.26
  12.7 38.1 %all-gather = bf16[1,1024,3,128]{3,1,2,0:T(8,128)(2,1)S(1)} all-gather(bf16[1,128,3,128]{3,1,2,0:T(8,128)(2,1)S(1)} %get-tuple-element.109), channel_id=2, replica_groups=mesh['rep'=2,'fsdp'=8,'tp'=8] {'fsdp'}, dimensions={1}, use_global_device_ids=true | all-gather | bytes 884736 | tf_op jit(solution)/shard_map/all_gather | solution.py:102
  57.1 31.6 %all-gather.1 = bf16[1,128,1024]{2,1,0:T(8,128)(2,1)S(1)} all-gather(bf16[1,128,128]{2,1,0:T(8,128)(2,1)S(1)} %get-tuple-element.111), channel_id=3, replica_groups=mesh['rep'=2,'fsdp'=8,'tp'=8] {'fsdp'}, dimensions={2}, use_global_device_ids=true | all-gather | bytes 294912 | tf_op jit(solution)/shard_map/all_gather | solution.py:103
  88.7 2.6 convolution_convert_fusion.1
  91.4 1.9 fusion.108
  97.5 63.3 %all-reduce.12.cloned.1.call-done = f32[577,1024]{1,0:T(8,128)} async-done(((f32[577,1024]{1,0:T(8,128)}), f32[577,1024]{1,0:T(8,128)}) %all-reduce.12.cloned.1.call-update) | async-done | bytes 2363408 | tf_op jit(solution)/shard_map/psum | solution.py:68
  160.8 2.4 fusion.150
  164.5 3.3 convolution_add_fusion.1
  167.8 23.0 %all-gather.15.cloned.1.call-done = bf16[1,512,1024]{2,1,0:T(8,128)(2,1)} async-done(((bf16[1,512,128]{2,1,0:T(8,128)(2,1)}), bf16[1,512,1024]{2,1,0:T(8,128)(2,1)}) %all-gather.15.cloned.1.call-update) | async-done | bytes 1048592 | tf_op jit(solution)/shard_map/all_gather | solution.py:105
  190.7 3.8 fusion.78
  197.2 32.9 %all-gather.5 = bf16[1,128,1024]{2,1,0:T(8,128)(2,1)} all-gather(bf16[1,128,128]{2,1,0:T(8,128)(2,1)S(1)} %get-tuple-element.110), channel_id=7, replica_groups=mesh['rep'=2,'fsdp'=8,'tp'=8] {'fsdp'}, dimensions={2}, use_global_device_ids=true | all-gather | bytes 294912 | tf_op jit(solution)/shard_map/all_gather | solution.py:103
  231.5 40.0 %all-gather.4 = bf16[1,1024,3,128]{3,1,2,0:T(8,128)(2,1)} all-gather(bf16[1,128,3,128]{3,1,2,0:T(8,128)(2,1)} %get-tuple-element.108), channel_id=6, replica_groups=mesh['rep'=2,'fsdp'=8,'tp'=8] {'fsdp'}, dimensions={1}, use_global_device_ids=true | all-gather | bytes 884736 | tf_op jit(solution)/shard_map/all_gather | solution.py:102
  271.4 2.0 fusion.149
  280.0 2.6 convolution_convert_fusion
  282.7 1.9 fusion.105
  286.0 62.3 %all-reduce.16.cloned.1.call-done = f32[577,1024]{1,0:T(8,128)} async-done(((f32[577,1024]{1,0:T(8,128)}), f32[577,1024]{1,0:T(8,128)}) %all-reduce.16.cloned.1.call-update) | async-done | bytes 2363408 | tf_op jit(solution)/shard_map/psum | solution.py:68
  348.3 2.8 fusion.148
  351.7 3.3 convolution_add_fusion
  355.1 23.3 %all-gather.19.cloned.1.call-done = bf16[1,512,1024]{2,1,0:T(8,128)(2,1)} async-done(((bf16[1,512,128]{2,1,0:T(8,128)(2,1)}), bf16[1,512,1024]{2,1,0:T(8,128)(2,1)}) %all-gather.19.cloned.1.call-update) | async-done | bytes 1048592 | tf_op jit(solution)/shard_map/all_gather | solution.py:105
  378.3 3.7 fusion.173
  382.9 2.2 fusion.74
  385.4 64.8 %all-reduce.18.cloned.1.call-done = f32[577,1024]{1,0:T(8,128)} async-done(((f32[577,1024]{1,0:T(8,128)}), f32[577,1024]{1,0:T(8,128)}) %all-reduce.18.cloned.1.call-update) | async-done | bytes 2363408 | tf_op jit(solution)/shard_map/psum | solution.py:72
  450.2 3.4 multiply_reduce_fusion.4
  459.5 3.4 fusion.118
  462.9 7.3 fusion.156
  470.2 6.8 fusion.68
  477.1 3.8 fusion.157
  485.9 3.6 convolution_bitcast_fusion.1
  489.6 66.3 %all-reduce.20.cloned.1.call-done = f32[577,1024]{1,0:T(8,128)} async-done(((f32[577,1024]{1,0:T(8,128)}), f32[577,1024]{1,0:T(8,128)}) %all-reduce.20.cloned.1.call-update) | async-done | bytes 2363408 | tf_op jit(solution)/shard_map/psum | solution.py:72
  555.9 4.1 multiply_reduce_fusion.6
  560.1 3.3 fusion.144
  563.3 1.7 fusion.174
  565.9 2.2 fusion.80
  568.3 3.0 fusion.95
  571.5 3.7 fusion.101
  575.4 4.1 fusion.56
  579.5 4.3 fusion.115
  583.9 51.4 %all-reduce.22.cloned.1.call-done = f32[577,1024]{1,0:T(8,128)} async-done(((f32[577,1024]{1,0:T(8,128)}), f32[577,1024]{1,0:T(8,128)}) %all-reduce.22.cloned.1.call-update) | async-done | bytes 2363408 | tf_op jit(solution)/shard_map/psum | solution.py:72
  635.3 4.1 multiply_reduce_fusion.5
  639.4 3.2 fusion.145
  645.3 4.5 fusion.98
  649.9 4.4 fusion.92
  654.6 2.8 convolution_convert_fusion.2
  659.2 3.3 fusion.116
  662.5 6.8 fusion.154
  670.0 6.3 fusion.65
  677.1 3.2 fusion.155
  680.5 3.9 fusion.114
  684.5 3.9 fusion.72
  688.4 2.3 convolution_bitcast_fusion
  693.3 29.4 %reduce-scatter.19.cloned.1.call-done = f32[128,512]{1,0:T(8,128)} async-done(((f32[1024,512]{1,0:T(8,128)}), f32[128,512]{1,0:T(8,128)}) %reduce-scatter.19.cloned.1.call-update) | async-done | bytes 262160 | tf_op jit(solution)/shard_map/reduce_scatter | solution.py:227
  722.7 78.4 %reduce-scatter.23.cloned.1.call-done = f32[512,128]{1,0:T(8,128)} async-done(((f32[512,1024]{1,0:T(8,128)}), f32[512,128]{1,0:T(8,128)}) %reduce-scatter.23.cloned.1.call-update) | async-done | bytes 262160 | tf_op jit(solution)/shard_map/reduce_scatter | solution.py:228
  801.0 76.5 %reduce-scatter.11.cloned.1.call-done = f32[128,3,128]{2,0,1:T(8,128)} async-done(((f32[1024,3,128]{2,0,1:T(8,128)}), f32[128,3,128]{2,0,1:T(8,128)}) %reduce-scatter.11.cloned.1.call-update) | async-done | bytes 196624 | tf_op jit(solution)/shard_map/reduce_scatter | solution.py:225
  877.5 73.4 %reduce-scatter.13.cloned.1.call-done = f32[128,128]{1,0:T(8,128)} async-done(((f32[128,1024]{1,0:T(8,128)}), f32[128,128]{1,0:T(8,128)}) %reduce-scatter.13.cloned.1.call-update) | async-done | bytes 65552 | tf_op jit(solution)/shard_map/reduce_scatter | solution.py:226
  950.9 79.1 %reduce-scatter.17.cloned.1.call-done = f32[128,512]{1,0:T(8,128)} async-done(((f32[1024,512]{1,0:T(8,128)}), f32[128,512]{1,0:T(8,128)}) %reduce-scatter.17.cloned.1.call-update) | async-done | bytes 262160 | tf_op jit(solution)/shard_map/reduce_scatter | solution.py:227
  1030.1 78.3 %reduce-scatter.21.cloned.1.call-done = f32[512,128]{1,0:T(8,128)} async-done(((f32[512,1024]{1,0:T(8,128)}), f32[512,128]{1,0:T(8,128)}) %reduce-scatter.21.cloned.1.call-update) | async-done | bytes 262160 | tf_op jit(solution)/shard_map/reduce_scatter | solution.py:228
  1108.4 76.7 %reduce-scatter.9.cloned.1.call-done = f32[128,3,128]{2,0,1:T(8,128)} async-done(((f32[1024,3,128]{2,0,1:T(8,128)}), f32[128,3,128]{2,0,1:T(8,128)}) %reduce-scatter.9.cloned.1.call-update) | async-done | bytes 196624 | tf_op jit(solution)/shard_map/reduce_scatter | solution.py:225
  1185.1 3.2 fusion.25
  1188.4 2.4 fusion.24
  1190.8 3.8 copy.79
  1195.3 3.8 copy.78
  1199.2 73.4 %all-reduce = (f32[2,1024]{1,0:T(2,128)}, f32[2,1024]{1,0:T(2,128)}, f32[2,2,128]{2,1,0:T(2,128)}, f32[2,1024]{1,0:T(2,128)}, f32[2,1024]{1,0:T(2,128)}, /*index...) all-reduce(f32[2,1024]{1,0:T(2,128)S(1)} %pad_maximum_fusion.10, ...), channel_id=1, replica_groups=mesh['rep'=2,'fsdp'=8,'tp'=8] {'rep','fsdp'}, use_global_device_ids=true, to_apply=%region_32.0 | all-reduce | flops 13824 | bytes 110592 | tf_op jit(solution)/shard_map/psum | solution.py:241
  1272.5 1.9 pad_maximum_fusion.1
  1274.4 1.9 pad_maximum_fusion
  (306 shorter events, 52.2 us)
Async XLA Ops:
  8.0 43.4 %copy-start.10 = (bf16[1,577,1024]{2,1,0:T(8,128)(2,1)S(1)}, bf16[1,577,1024]{2,1,0:T(8,128)(2,1)}, u32[]{:S(2)}) copy-start(bf16[1,577,1024]{2,1,0:T(8,128)(2,1)} %param.14) | copy-start | bytes 3545092
  8.0 3.4 copy-start.64
  8.0 4.1 copy-start.42
  8.0 42.8 %copy-start.65 = (f32[2,1024]{1,0:T(2,128)S(1)}, f32[2,1024]{1,0:T(2,128)}, u32[]{:S(2)}) copy-start(f32[2,1024]{1,0:T(2,128)} %param.17) | copy-start | bytes 24580
  8.1 152.7 %all-reduce.12.cloned.1.call-start = ((), (), s32[]{:S(2)}) async-start(), calls=%async_computation.8 | async-start | bytes 4784128 | tf_op jit(solution)/shard_map/psum | solution.py:68
  11.5 41.1 %copy-start.47 = (f32[577]{0:T(1024)}, f32[577]{0:T(1024)S(1)}, u32[]{:S(2)}) copy-start(f32[577]{0:T(1024)S(1)} %add_rsqrt_fusion.3) | copy-start | bytes 6928
  12.1 40.5 %copy-start.50 = (f32[1,1024]{1,0:T(1,128)}, f32[1,1024]{1,0:T(1,128)S(1)}, u32[]{:S(2)}) copy-start(f32[1,1024]{1,0:T(1,128)S(1)} %get-tuple-element.119) | copy-start | bytes 12292
  52.8 4.0 copy-start.27
  53.3 3.5 copy-start.32
  57.1 36.2 %copy-start.69 = (f32[2,64]{1,0:T(2,128)}, f32[2,64]{1,0:T(2,128)S(1)}, u32[]{:S(2)}) copy-start(f32[2,64]{1,0:T(2,128)S(1)} %add.304) | copy-start | bytes 1540
  88.7 4.6 copy-start.20
  93.3 3.5 copy-start.68
  93.4 71.1 %all-gather.13.cloned.1.call-start = ((), (), s32[]{:S(2)}) async-start(), calls=%async_computation.22 | async-start | bytes 1179648 | tf_op jit(solution)/shard_map/all_gather | solution.py:104
  94.2 96.5 %all-gather.15.cloned.1.call-start = ((), (), s32[]{:S(2)}) async-start(), calls=%async_computation.23 | async-start | bytes 1179648 | tf_op jit(solution)/shard_map/all_gather | solution.py:105
  95.0 176.4 %all-reduce.14.cloned.1.call-start = ((), (), s32[]{:S(2)}) async-start(), calls=%async_computation.9 | async-start | bytes 4784128 | tf_op jit(solution)/shard_map/psum | solution.py:68
  163.2 108.3 %copy-start = (f32[577,1024]{1,0:T(8,128)}, f32[577,1024]{1,0:T(8,128)S(1)}, u32[]{:S(2)}) copy-start(f32[577,1024]{1,0:T(8,128)S(1)} %get-tuple-element.91) | copy-start | bytes 7090180
  194.6 153.7 %all-reduce.16.cloned.1.call-start = ((), (), s32[]{:S(2)}) async-start(), calls=%async_computation.10 | async-start | bytes 4784128 | tf_op jit(solution)/shard_map/psum | solution.py:68
  276.5 3.3 copy-start.28
  280.0 4.6 copy-start.18
  282.7 65.6 %copy-start.58 = (f32[1,1024]{1,0:T(1,128)S(1)}, f32[1,1024]{1,0:T(1,128)}, u32[]{:S(2)}) copy-start(f32[1,1024]{1,0:T(1,128)} %get-tuple-element.123) | copy-start | bytes 12292
  284.6 66.8 %all-gather.17.cloned.1.call-start = ((), (), s32[]{:S(2)}) async-start(), calls=%async_computation.24 | async-start | bytes 1179648 | tf_op jit(solution)/shard_map/all_gather | solution.py:104
  285.2 93.1 %all-gather.19.cloned.1.call-start = ((), (), s32[]{:S(2)}) async-start(), calls=%async_computation.25 | async-start | bytes 1179648 | tf_op jit(solution)/shard_map/all_gather | solution.py:105
  286.0 164.3 %all-reduce.18.cloned.1.call-start = ((), (), s32[]{:S(2)}) async-start(), calls=%async_computation.11 | async-start | bytes 4784128 | tf_op jit(solution)/shard_map/psum | solution.py:72
  378.3 4.6 copy-start.31
  385.2 170.7 %all-reduce.20.cloned.1.call-start = ((), (), s32[]{:S(2)}) async-start(), calls=%async_computation.12 | async-start | bytes 4784128 | tf_op jit(solution)/shard_map/psum | solution.py:72
  450.2 3.4 copy-start.14
  450.2 3.4 copy-start.15
  489.6 145.7 %all-reduce.22.cloned.1.call-start = ((), (), s32[]{:S(2)}) async-start(), calls=%async_computation.13 | async-start | bytes 4784128 | tf_op jit(solution)/shard_map/psum | solution.py:72
  555.9 4.1 copy-start.3
  555.9 4.1 copy-start.7
  560.0 3.3 copy-start.16
  568.2 3.3 copy-start.78
  568.2 125.0 %reduce-scatter.15.cloned.1.call-start = ((), (), s32[]{:S(2)}) async-start(), calls=%async_computation.17 | async-start | bytes 589824 | tf_op jit(solution)/shard_map/reduce_scatter | solution.py:226
  571.3 151.4 %reduce-scatter.19.cloned.1.call-start = ((), (), s32[]{:S(2)}) async-start(), calls=%async_computation.19 | async-start | bytes 2359296 | tf_op jit(solution)/shard_map/reduce_scatter | solution.py:227
  575.3 4.2 copy-start.76
  575.3 225.7 %reduce-scatter.23.cloned.1.call-start = ((), (), s32[]{:S(2)}) async-start(), calls=%async_computation.21 | async-start | bytes 2359296 | tf_op jit(solution)/shard_map/reduce_scatter | solution.py:228
  579.5 55.8 %copy-start.49 = (f32[577]{0:T(1024)S(1)}, f32[577]{0:T(1024)}, u32[]{:S(2)}) copy-start(f32[577]{0:T(1024)} %add_rsqrt_fusion.2) | copy-start | bytes 6928
  579.5 55.8 %copy-start.53 = (f32[1,1024]{1,0:T(1,128)S(1)}, f32[1,1024]{1,0:T(1,128)}, u32[]{:S(2)}) copy-start(f32[1,1024]{1,0:T(1,128)} %get-tuple-element.115) | copy-start | bytes 12292
  579.5 298.0 %reduce-scatter.11.cloned.1.call-start = ((), (), s32[]{:S(2)}) async-start(), calls=%async_computation.15 | async-start | bytes 1769472 | tf_op jit(solution)/shard_map/reduce_scatter | solution.py:225
  583.8 367.1 %reduce-scatter.13.cloned.1.call-start = ((), (), s32[]{:S(2)}) async-start(), calls=%async_computation.16 | async-start | bytes 589824 | tf_op jit(solution)/shard_map/reduce_scatter | solution.py:226
  635.3 4.1 copy-start.1
  635.3 4.1 copy-start.13
  639.4 4.6 copy-start.24
  645.3 384.8 %reduce-scatter.17.cloned.1.call-start = ((), (), s32[]{:S(2)}) async-start(), calls=%async_computation.18 | async-start | bytes 2359296 | tf_op jit(solution)/shard_map/reduce_scatter | solution.py:227
  649.8 458.6 %reduce-scatter.21.cloned.1.call-start = ((), (), s32[]{:S(2)}) async-start(), calls=%async_computation.20 | async-start | bytes 2359296 | tf_op jit(solution)/shard_map/reduce_scatter | solution.py:228
  654.3 4.9 copy-start.70
  654.3 530.8 %reduce-scatter.9.cloned.1.call-start = ((), (), s32[]{:S(2)}) async-start(), calls=%async_computation.14 | async-start | bytes 1769472 | tf_op jit(solution)/shard_map/reduce_scatter | solution.py:225
  662.5 7.6 copy-start.83
  670.0 7.1 copy-start.26
  676.3 4.1 copy-start.48
  676.3 4.1 copy-start.51
  676.3 4.1 copy-start.74
  680.5 3.9 copy-start.36
  684.4 4.0 copy-start.34
  684.4 4.0 copy-start.35
  684.4 500.7 %all-reduce.24.cloned.1.call-start = ((), (), s32[]{:S(2)}) async-start(), calls=%async_computation.26 | async-start | bytes 9568256 | tf_op jit(solution)/shard_map/psum | solution.py:68
  684.5 3.9 copy-start.37
  690.8 581.7 %all-reduce.26.cloned.1.call-start = ((), (), s32[]{:S(2)}) async-start(), calls=%async_computation.27 | async-start | bytes 3145728 | tf_op jit(solution)/shard_map/psum | solution.py:230
  1190.8 3.9 copy-start.19
  1190.8 3.9 copy-start.55
  1195.2 3.9 copy-start.60
  1195.3 3.9 copy-start.59
  1272.5 5.3 copy-start.43
  1272.5 5.3 copy-start.44
  (45 other events, 90.9 us)
Sparse Core Ops, SparseCore 0:
  93.5 67.2 all-reduce.11
  194.7 65.6 all-reduce.13
  284.8 63.4 all-reduce.15
  385.3 64.8 all-reduce.17
  489.7 66.1 all-reduce.19
  568.3 66.8 all-reduce.21
  691.0 75.1 all-reduce.23
  1185.2 59.1 all-reduce.25
Sparse Core Ops, SparseCore 1:
  97.1 46.6 all-gather.12
  146.6 44.1 all-gather.14
  288.3 42.8 all-gather.16
  334.2 44.1 all-gather.18
  573.1 70.1 reduce-scatter.14
  648.0 74.6 reduce-scatter.18
  726.7 74.3 reduce-scatter.22
  805.0 72.4 reduce-scatter.10
  881.5 69.4 reduce-scatter.12
  955.7 74.3 reduce-scatter.16
  1034.1 74.2 reduce-scatter.20
  1112.5 72.5 reduce-scatter.8
where the time goes:
time: 1290 us
  waiting for transfers between devices  848 us (66%)
  blocking collectives  216 us (17%)
  matrix products  117 us (9%)
  other arithmetic  47.2 us (4%)
  local copies, waits for them, and re-layouts  39.8 us (3%)
  between operations  17.3 us (1%)
    psum x3, waiting for transfers between devices, input_total(): return lax.psum(contrib, 'tp')  182 us
    reduce_scatter x2, waiting for transfers between devices, body(): lax.psum_scatter(d_down, 'fsdp', scatter_dimension=1, tiled=True)  157 us
    reduce_scatter x2, waiting for transfers between devices, body(): lax.psum_scatter(d_qkv, 'fsdp', scatter_dimension=0, tiled=True)  153 us
    psum x4, waiting for transfers between devices, branch_total(): return lax.psum(contrib, 'tp')  126 us
    reduce_scatter x2, waiting for transfers between devices, body(): lax.psum_scatter(d_up, 'fsdp', scatter_dimension=0, tiled=True)  109 us
    all_gather x2, blocking collectives, body(): lax.all_gather(qkv_weight[layer_idx], 'fsdp', axis=0, tiled=True)  78.1 us
    reduce_scatter x2, waiting for transfers between devices, body(): lax.psum_scatter(d_out, 'fsdp', scatter_dimension=1, tiled=True)  73.4 us
    psum x1, blocking collectives, body(): lax.psum((small_stack[0], small_stack[1], small_stack[2], small_stack[3],...  73.4 us
  transfers between devices with their start and end apart: 20, of which 14 were waited for; matrix products, arithmetic and copies ran while one was open for 8% of the time, Pallas kernels for 0%

commit v1 on v0

--- a/solution.py
+++ b/solution.py
@@ -69,7 +69,7 @@
 
 
 def input_total(contrib):
-    return lax.psum(contrib, "tp")
+    return jnp.sum(lax.all_gather(contrib, "tp"), axis=0)
 
 
 def body(

time: 1290 us -> 1530 us (1.19)
  waiting for transfers between devices: 848 us -> 1040 us
  other arithmetic: 47.2 us -> 93.2 us
    all_gather x0 -> x4, waiting for transfers between devices: none -> 282 us  [input_total(): return jnp.sum(lax.all_gather(contrib, 'tp'), axis=0)]
    psum x3 -> x0, waiting for transfers between devices: 182 us -> none  [input_total(): return lax.psum(contrib, 'tp')]
    reduce_scatter x2, waiting for transfers between devices: 73.4 us -> 147 us  [body(): lax.psum_scatter(d_out, 'fsdp', scatter_dimension=1, tiled=True)]
    reduce_scatter x2, waiting for transfers between devices: 157 us -> 99.9 us  [body(): lax.psum_scatter(d_down, 'fsdp', scatter_dimension=1, tiled=True)]
    psum x4, waiting for transfers between devices: 126 us -> 179 us  [branch_total(): return lax.psum(contrib, 'tp')]
    psum x1, waiting for transfers between devices: 0.01 us -> 52.1 us  [body(): lax.psum((shares[0], shares[1], shares[2], shares[3]), 'rep')]
    reduce_sum x0 -> x4, other arithmetic: none -> 44.9 us  [the longest x2 22.5 us: body(): d_shift_two = jnp.sum(d_norm_two, 0)]
    reduce_scatter x2, waiting for transfers between devices: 109 us -> 78.6 us  [body(): lax.psum_scatter(d_up, 'fsdp', scatter_dimension=0, tiled=True)]
  transfers between devices with their start and end apart: 20 -> 21, of which waited for: 14 -> 17; matrix products, arithmetic and copies ran while one was open for 8% -> 8% of each run, Pallas kernels for 0% -> 0%
where the time goes in v1:
time: 1530 us; the launch traced here: 1520 us
  waiting for transfers between devices  1040 us (68%)
  blocking collectives  216 us (14%)
  matrix products  110 us (7%)
  other arithmetic  93.2 us (6%)
  local copies, waits for them, and re-layouts  46.3 us (3%)
  between operations  17.1 us (1%)
    all_gather x4, waiting for transfers between devices, input_total(): return jnp.sum(lax.all_gather(contrib, 'tp'), axis=0)  282 us
    psum x4, waiting for transfers between devices, branch_total(): return lax.psum(contrib, 'tp')  179 us
    reduce_scatter x2, waiting for transfers between devices, body(): lax.psum_scatter(d_qkv, 'fsdp', scatter_dimension=0, tiled=True)  154 us
    reduce_scatter x2, waiting for transfers between devices, body(): lax.psum_scatter(d_out, 'fsdp', scatter_dimension=1, tiled=True)  147 us
    reduce_scatter x2, waiting for transfers between devices, body(): lax.psum_scatter(d_down, 'fsdp', scatter_dimension=1, tiled=True)  99.9 us
    reduce_scatter x2, waiting for transfers between devices, body(): lax.psum_scatter(d_up, 'fsdp', scatter_dimension=0, tiled=True)  78.6 us
    all_gather x2, blocking collectives, body(): lax.all_gather(qkv_weight[layer_idx], 'fsdp', axis=0, tiled=True)  76.3 us
    psum x1, blocking collectives, body(): lax.psum((small_stack[0], small_stack[1], small_stack[2], small_stack[3],...  75.3 us
  transfers between devices with their start and end apart: 21, of which 17 were waited for; matrix products, arithmetic and copies ran while one was open for 8% of the time, Pallas kernels for 0%

profile of v1, /device:TPU:0, one launch (start us, length us, event | category | flops | bytes accessed | tf_op | source)
XLA Modules:
  0.0 1523.2 jit_solution(12934431218995740970)
XLA Ops:
  12.7 38.1 %all-gather = bf16[1,1024,3,128]{3,1,2,0:T(8,128)(2,1)S(1)} all-gather(bf16[1,128,3,128]{3,1,2,0:T(8,128)(2,1)S(1)} %get-tuple-element.126), channel_id=2, replica_groups=mesh['rep'=2,'fsdp'=8,'tp'=8] {'fsdp'}, dimensions={1}, use_global_device_ids=true | all-gather | bytes 884736 | tf_op jit(solution)/shard_map/all_gather | solution.py:102
  57.9 31.6 %all-gather.1 = bf16[1,128,1024]{2,1,0:T(8,128)(2,1)S(1)} all-gather(bf16[1,128,128]{2,1,0:T(8,128)(2,1)S(1)} %get-tuple-element.128), channel_id=3, replica_groups=mesh['rep'=2,'fsdp'=8,'tp'=8] {'fsdp'}, dimensions={2}, use_global_device_ids=true | all-gather | bytes 294912 | tf_op jit(solution)/shard_map/all_gather | solution.py:103
  96.3 63.3 %all-reduce.8.cloned.1.call-done = f32[577,1024]{1,0:T(8,128)} async-done(((f32[577,1024]{1,0:T(8,128)}), f32[577,1024]{1,0:T(8,128)}) %all-reduce.8.cloned.1.call-update) | async-done | bytes 2363408 | tf_op jit(solution)/shard_map/psum | solution.py:68
  159.6 2.4 fusion.152
  162.5 3.3 convolution_add_fusion.1
  165.8 23.8 %all-gather.27.cloned.1.call-done = bf16[1,512,1024]{2,1,0:T(8,128)(2,1)} async-done(((bf16[1,512,128]{2,1,0:T(8,128)(2,1)}), bf16[1,512,1024]{2,1,0:T(8,128)(2,1)}) %all-gather.27.cloned.1.call-update) | async-done | bytes 1048592 | tf_op jit(solution)/shard_map/all_gather | solution.py:105
  189.6 3.8 fusion.77
  194.7 32.9 %all-gather.5 = bf16[1,128,1024]{2,1,0:T(8,128)(2,1)} all-gather(bf16[1,128,128]{2,1,0:T(8,128)(2,1)S(1)} %get-tuple-element.127), channel_id=7, replica_groups=mesh['rep'=2,'fsdp'=8,'tp'=8] {'fsdp'}, dimensions={2}, use_global_device_ids=true | all-gather | bytes 294912 | tf_op jit(solution)/shard_map/all_gather | solution.py:103
  228.3 38.2 %all-gather.4 = bf16[1,1024,3,128]{3,1,2,0:T(8,128)(2,1)S(1)} all-gather(bf16[1,128,3,128]{3,1,2,0:T(8,128)(2,1)} %get-tuple-element.125), channel_id=6, replica_groups=mesh['rep'=2,'fsdp'=8,'tp'=8] {'fsdp'}, dimensions={1}, use_global_device_ids=true | all-gather | bytes 884736 | tf_op jit(solution)/shard_map/all_gather | solution.py:102
  266.5 2.0 fusion.151
  281.2 2.7 convolution_convert_fusion
  284.5 1.9 fusion.103
  287.8 62.1 %all-reduce.12.cloned.1.call-done = f32[577,1024]{1,0:T(8,128)} async-done(((f32[577,1024]{1,0:T(8,128)}), f32[577,1024]{1,0:T(8,128)}) %all-reduce.12.cloned.1.call-update) | async-done | bytes 2363408 | tf_op jit(solution)/shard_map/psum | solution.py:68
  349.9 2.8 fusion.150
  354.6 4.0 convolution_add_fusion
  358.6 20.9 %all-gather.31.cloned.1.call-done = bf16[1,512,1024]{2,1,0:T(8,128)(2,1)} async-done(((bf16[1,512,128]{2,1,0:T(8,128)(2,1)}), bf16[1,512,1024]{2,1,0:T(8,128)(2,1)}) %all-gather.31.cloned.1.call-update) | async-done | bytes 1048592 | tf_op jit(solution)/shard_map/all_gather | solution.py:105
  379.5 3.7 fusion.175
  384.0 2.2 convolution_bitcast_fusion.3
  386.4 3.9 fusion.72
  390.5 89.0 %all-gather.33.cloned.1.call-done = f32[8,577,1024]{2,1,0:T(8,128)} async-done(((f32[1,577,1024]{2,1,0:T(8,128)}), f32[8,577,1024]{2,1,0:T(8,128)}) %all-gather.33.cloned.1.call-update) | async-done | bytes 18907152 | tf_op jit(solution)/shard_map/all_gather | solution.py:72
  479.4 11.2 fusion.143
  490.7 3.9 multiply_reduce_fusion.4
  495.2 54.1 %all-reduce.14.cloned.1.call-done = f32[577,1024]{1,0:T(8,128)} async-done(((f32[577,1024]{1,0:T(8,128)}), f32[577,1024]{1,0:T(8,128)}) %all-reduce.14.cloned.1.call-update) | async-done | bytes 2363408 | tf_op jit(solution)/shard_map/psum | solution.py:68
  549.3 5.8 fusion.148
  559.3 3.4 fusion.116
  562.7 7.3 fusion.158
  570.0 6.8 fusion.68
  576.8 3.8 fusion.159
  585.7 3.3 convolution_bitcast_fusion.2
  589.3 94.2 %all-gather.35.cloned.1.call-done = f32[8,577,1024]{2,1,0:T(8,128)} async-done(((f32[1,577,1024]{2,1,0:T(8,128)}), f32[8,577,1024]{2,1,0:T(8,128)}) %all-gather.35.cloned.1.call-update) | async-done | bytes 18907152 | tf_op jit(solution)/shard_map/all_gather | solution.py:72
  683.4 11.2 fusion.145
  694.7 4.1 multiply_reduce_fusion.6
  698.8 3.3 fusion.146
  704.6 2.2 convolution_bitcast_fusion.1
  707.0 4.4 fusion.99
  711.4 4.0 fusion.56
  715.6 3.4 fusion.93
  719.1 4.6 fusion.113
  724.3 3.7 fusion.96
  728.1 4.4 fusion.90
  732.6 70.0 %all-gather.37.cloned.1.call-done = f32[8,577,1024]{2,1,0:T(8,128)} async-done(((f32[1,577,1024]{2,1,0:T(8,128)}), f32[8,577,1024]{2,1,0:T(8,128)}) %all-gather.37.cloned.1.call-update) | async-done | bytes 18907152 | tf_op jit(solution)/shard_map/all_gather | solution.py:72
  802.6 11.3 fusion.142
  813.9 2.8 multiply_reduce_fusion.5
  820.2 2.9 fusion.87
  823.1 2.4 fusion.114
  825.6 5.7 fusion.156
  833.0 5.0 fusion.65
  840.7 3.8 fusion.112
  844.6 21.9 %reduce-scatter.23.cloned.1.call-done = f32[512,128]{1,0:T(8,128)} async-done(((f32[512,1024]{1,0:T(8,128)}), f32[512,128]{1,0:T(8,128)}) %reduce-scatter.23.cloned.1.call-update) | async-done | bytes 262160 | tf_op jit(solution)/shard_map/reduce_scatter | solution.py:228
  866.5 73.3 %reduce-scatter.15.cloned.1.call-done = f32[128,128]{1,0:T(8,128)} async-done(((f32[128,1024]{1,0:T(8,128)}), f32[128,128]{1,0:T(8,128)}) %reduce-scatter.15.cloned.1.call-update) | async-done | bytes 65552 | tf_op jit(solution)/shard_map/reduce_scatter | solution.py:226
  939.8 76.7 %reduce-scatter.11.cloned.1.call-done = f32[128,3,128]{2,0,1:T(8,128)} async-done(((f32[1024,3,128]{2,0,1:T(8,128)}), f32[128,3,128]{2,0,1:T(8,128)}) %reduce-scatter.11.cloned.1.call-update) | async-done | bytes 196624 | tf_op jit(solution)/shard_map/reduce_scatter | solution.py:225
  1016.6 78.5 %reduce-scatter.17.cloned.1.call-done = f32[128,512]{1,0:T(8,128)} async-done(((f32[1024,512]{1,0:T(8,128)}), f32[128,512]{1,0:T(8,128)}) %reduce-scatter.17.cloned.1.call-update) | async-done | bytes 262160 | tf_op jit(solution)/shard_map/reduce_scatter | solution.py:227
  1095.1 78.0 %reduce-scatter.21.cloned.1.call-done = f32[512,128]{1,0:T(8,128)} async-done(((f32[512,1024]{1,0:T(8,128)}), f32[512,128]{1,0:T(8,128)}) %reduce-scatter.21.cloned.1.call-update) | async-done | bytes 262160 | tf_op jit(solution)/shard_map/reduce_scatter | solution.py:228
  1173.1 73.3 %reduce-scatter.13.cloned.1.call-done = f32[128,128]{1,0:T(8,128)} async-done(((f32[128,1024]{1,0:T(8,128)}), f32[128,128]{1,0:T(8,128)}) %reduce-scatter.13.cloned.1.call-update) | async-done | bytes 65552 | tf_op jit(solution)/shard_map/reduce_scatter | solution.py:226
  1246.4 77.0 %reduce-scatter.9.cloned.1.call-done = f32[128,3,128]{2,0,1:T(8,128)} async-done(((f32[1024,3,128]{2,0,1:T(8,128)}), f32[128,3,128]{2,0,1:T(8,128)}) %reduce-scatter.9.cloned.1.call-update) | async-done | bytes 196624 | tf_op jit(solution)/shard_map/reduce_scatter | solution.py:225
  1323.6 2.2 convolution_bitcast_fusion
  1327.9 3.8 copy.102
  1332.1 52.1 %all-reduce.16.cloned.1.call-done = (f32[1,128,3,128]{3,1,2,0:T(8,128)}, f32[1,128,3,128]{3,1,2,0:T(8,128)}, f32[1,128,128]{2,1,0:T(8,128)}, f32[1,128,128]{2,1,...) async-done(((f32[1,128,3,128]{3,1,2,0:T(8,128)}, f32[1,128,3,128]{3,1,2,0:T(8,128)}, ...) | async-done | bytes 1572880 | tf_op jit(solution)/shard_map/psum | solution.py:230
  1391.3 28.4 %all-gather.39.cloned.1.call-done = f32[8,577,1024]{2,1,0:T(8,128)} async-done(((f32[1,577,1024]{2,1,0:T(8,128)}), f32[8,577,1024]{2,1,0:T(8,128)}) %all-gather.39.cloned.1.call-update) | async-done | bytes 18907152 | tf_op jit(solution)/shard_map/all_gather | solution.py:72
  1419.7 11.2 fusion.144
  1430.9 2.8 fusion.25
  1433.8 2.5 fusion.24
  1436.3 3.8 copy.103
  1440.2 75.3 %all-reduce = (f32[2,1024]{1,0:T(2,128)}, f32[2,1024]{1,0:T(2,128)}, f32[2,2,128]{2,1,0:T(2,128)}, f32[2,1024]{1,0:T(2,128)}, f32[2,1024]{1,0:T(2,128)}, /*index...) all-reduce(f32[2,1024]{1,0:T(2,128)S(1)} %pad_maximum_fusion.10, ...), channel_id=1, replica_groups=mesh['rep'=2,'fsdp'=8,'tp'=8] {'rep','fsdp'}, use_global_device_ids=true, to_apply=%region_32.0 | all-reduce | flops 13824 | bytes 110592 | tf_op jit(solution)/shard_map/psum | solution.py:241
  (312 shorter events, 69.4 us)
Async XLA Ops:
  8.0 43.5 %copy-start.10 = (bf16[1,577,1024]{2,1,0:T(8,128)(2,1)S(1)}, bf16[1,577,1024]{2,1,0:T(8,128)(2,1)}, u32[]{:S(2)}) copy-start(bf16[1,577,1024]{2,1,0:T(8,128)(2,1)} %param.14) | copy-start | bytes 3545092
  8.0 3.4 copy-start.61
  8.0 4.1 copy-start.43
  8.0 42.8 %copy-start.62 = (f32[2,1024]{1,0:T(2,128)S(1)}, f32[2,1024]{1,0:T(2,128)}, u32[]{:S(2)}) copy-start(f32[2,1024]{1,0:T(2,128)} %param.17) | copy-start | bytes 24580
  8.1 151.5 %all-reduce.8.cloned.1.call-start = ((), (), s32[]{:S(2)}) async-start(), calls=%async_computation.8 | async-start | bytes 4784128 | tf_op jit(solution)/shard_map/psum | solution.py:68
  11.5 41.1 %copy-start.44 = (f32[577]{0:T(1024)}, f32[577]{0:T(1024)S(1)}, u32[]{:S(2)}) copy-start(f32[577]{0:T(1024)S(1)} %add_rsqrt_fusion.3) | copy-start | bytes 6928
  12.1 40.5 %copy-start.48 = (f32[1,1024]{1,0:T(1,128)}, f32[1,1024]{1,0:T(1,128)S(1)}, u32[]{:S(2)}) copy-start(f32[1,1024]{1,0:T(1,128)S(1)} %get-tuple-element.136) | copy-start | bytes 12292
  55.1 35.1 %copy-start.2 = (f32[2,577,577]{1,2,0:T(8,128)}, f32[2,577,577]{1,2,0:T(8,128)S(1)}, u32[]{:S(2)}) copy-start(f32[2,577,577]{1,2,0:T(8,128)S(1)} %get-tuple-element.144) | copy-start | bytes 7990300
  57.2 35.1 %copy-start.67 = (f32[2,64]{1,0:T(2,128)}, f32[2,64]{1,0:T(2,128)S(1)}, u32[]{:S(2)}) copy-start(f32[2,64]{1,0:T(2,128)S(1)} %add.296) | copy-start | bytes 1540
  92.2 3.5 copy-start.65
  92.3 70.2 %all-gather.25.cloned.1.call-start = ((), (), s32[]{:S(2)}) async-start(), calls=%async_computation.20 | async-start | bytes 1179648 | tf_op jit(solution)/shard_map/all_gather | solution.py:104
  93.1 96.5 %all-gather.27.cloned.1.call-start = ((), (), s32[]{:S(2)}) async-start(), calls=%async_computation.21 | async-start | bytes 1179648 | tf_op jit(solution)/shard_map/all_gather | solution.py:105
  93.9 172.6 %all-reduce.10.cloned.1.call-start = ((), (), s32[]{:S(2)}) async-start(), calls=%async_computation.9 | async-start | bytes 4784128 | tf_op jit(solution)/shard_map/psum | solution.py:68
  95.1 67.3 %copy-start.51 = (f32[1,1024]{1,0:T(1,128)}, f32[1,1024]{1,0:T(1,128)S(1)}, u32[]{:S(2)}) copy-start(f32[1,1024]{1,0:T(1,128)S(1)} %get-tuple-element.132) | copy-start | bytes 12292
  96.3 66.2 %copy-start.75 = (f32[1,1024]{1,0:T(1,128)}, f32[1,1024]{1,0:T(1,128)S(1)}, u32[]{:S(2)}) copy-start(f32[1,1024]{1,0:T(1,128)S(1)} %get-tuple-element.134) | copy-start | bytes 12292
  165.8 27.7 %copy-start.86 = (f32[128]{0:T(128)S(1)}, f32[128]{0:T(128)}, u32[]{:S(2)}) copy-start(f32[128]{0:T(128)} %get-tuple-element.79) | copy-start | bytes 1540
  165.8 28.4 %copy-start.85 = (f32[128]{0:T(128)S(1)}, f32[128]{0:T(128)}, u32[]{:S(2)}) copy-start(f32[128]{0:T(128)} %get-tuple-element.76) | copy-start | bytes 1540
  193.4 34.3 %copy-start.66 = (f32[2,1024]{1,0:T(2,128)S(1)}, f32[2,1024]{1,0:T(2,128)}, u32[]{:S(2)}) copy-start(f32[2,1024]{1,0:T(2,128)} %param.27) | copy-start | bytes 24580
  193.4 156.6 %all-reduce.12.cloned.1.call-start = ((), (), s32[]{:S(2)}) async-start(), calls=%async_computation.10 | async-start | bytes 4784128 | tf_op jit(solution)/shard_map/psum | solution.py:68
  270.3 5.1 copy-start.84
  277.2 4.0 copy-start.69
  284.5 65.4 %copy-start.60 = (f32[1,1024]{1,0:T(1,128)S(1)}, f32[1,1024]{1,0:T(1,128)}, u32[]{:S(2)}) copy-start(f32[1,1024]{1,0:T(1,128)} %get-tuple-element.140) | copy-start | bytes 12292
  286.4 68.1 %all-gather.29.cloned.1.call-start = ((), (), s32[]{:S(2)}) async-start(), calls=%async_computation.22 | async-start | bytes 1179648 | tf_op jit(solution)/shard_map/all_gather | solution.py:104
  287.0 92.5 %all-gather.31.cloned.1.call-start = ((), (), s32[]{:S(2)}) async-start(), calls=%async_computation.23 | async-start | bytes 1179648 | tf_op jit(solution)/shard_map/all_gather | solution.py:105
  287.8 191.7 %all-gather.33.cloned.1.call-start = ((), (), s32[]{:S(2)}) async-start(), calls=%async_computation.24 | async-start | bytes 21528576 | tf_op jit(solution)/shard_map/all_gather | solution.py:72
  379.5 4.6 copy-start.31
  386.3 162.9 %all-reduce.14.cloned.1.call-start = ((), (), s32[]{:S(2)}) async-start(), calls=%async_computation.11 | async-start | bytes 4784128 | tf_op jit(solution)/shard_map/psum | solution.py:68
  390.3 293.2 %all-gather.35.cloned.1.call-start = ((), (), s32[]{:S(2)}) async-start(), calls=%async_computation.25 | async-start | bytes 21528576 | tf_op jit(solution)/shard_map/all_gather | solution.py:72
  549.3 7.2 copy-start.22
  589.0 213.6 %all-gather.37.cloned.1.call-start = ((), (), s32[]{:S(2)}) async-start(), calls=%async_computation.26 | async-start | bytes 21528576 | tf_op jit(solution)/shard_map/all_gather | solution.py:72
  694.7 4.1 copy-start.1
  694.7 4.1 copy-start.9
  706.9 137.7 %reduce-scatter.19.cloned.1.call-start = ((), (), s32[]{:S(2)}) async-start(), calls=%async_computation.17 | async-start | bytes 2359296 | tf_op jit(solution)/shard_map/reduce_scatter | solution.py:227
  711.4 4.2 copy-start.26
  711.4 155.1 %reduce-scatter.23.cloned.1.call-start = ((), (), s32[]{:S(2)}) async-start(), calls=%async_computation.19 | async-start | bytes 2359296 | tf_op jit(solution)/shard_map/reduce_scatter | solution.py:228
  715.5 3.6 copy-start.33
  715.5 3.6 copy-start.34
  715.5 3.6 copy-start.35
  715.5 3.6 copy-start.74
  715.5 224.3 %reduce-scatter.15.cloned.1.call-start = ((), (), s32[]{:S(2)}) async-start(), calls=%async_computation.15 | async-start | bytes 589824 | tf_op jit(solution)/shard_map/reduce_scatter | solution.py:226
  719.0 5.3 copy-start.47
  719.0 5.3 copy-start.52
  719.0 5.3 copy-start.76
  719.0 297.6 %reduce-scatter.11.cloned.1.call-start = ((), (), s32[]{:S(2)}) async-start(), calls=%async_computation.13 | async-start | bytes 1769472 | tf_op jit(solution)/shard_map/reduce_scatter | solution.py:225
  723.8 371.4 %reduce-scatter.17.cloned.1.call-start = ((), (), s32[]{:S(2)}) async-start(), calls=%async_computation.16 | async-start | bytes 2359296 | tf_op jit(solution)/shard_map/reduce_scatter | solution.py:227
  728.1 445.0 %reduce-scatter.21.cloned.1.call-start = ((), (), s32[]{:S(2)}) async-start(), calls=%async_computation.18 | async-start | bytes 2359296 | tf_op jit(solution)/shard_map/reduce_scatter | solution.py:228
  732.6 513.8 %reduce-scatter.13.cloned.1.call-start = ((), (), s32[]{:S(2)}) async-start(), calls=%async_computation.14 | async-start | bytes 589824 | tf_op jit(solution)/shard_map/reduce_scatter | solution.py:226
  825.5 7.5 copy-start.28
  825.5 7.5 copy-start.82
  825.5 497.8 %reduce-scatter.9.cloned.1.call-start = ((), (), s32[]{:S(2)}) async-start(), calls=%async_computation.12 | async-start | bytes 1769472 | tf_op jit(solution)/shard_map/reduce_scatter | solution.py:225
  844.5 479.1 %copy-start.18 = (bf16[1,1024,3,128]{3,1,2,0:T(8,128)(2,1)S(1)}, bf16[1,1024,3,128]{3,1,2,0:T(8,128)(2,1)}, u32[]{:S(2)}) copy-start(bf16[1,1024,3,128]{3,1,2,0:T(8,128)(2,1)} %copy-done.17) | copy-start | bytes 2359300
  844.5 479.1 %copy-start.37 = (bf16[577,1,128]{2,0,1:T(8,128)(2,1)S(1)}, bf16[577,1,128]{2,0,1:T(8,128)(2,1)}, u32[]{:S(2)}) copy-start(bf16[577,1,128]{2,0,1:T(8,128)(2,1)} %copy.100) | copy-start | bytes 443140
  844.5 539.7 %all-reduce.16.cloned.1.call-start = ((), (), s32[]{:S(2)}) async-start(), calls=%async_computation.28 | async-start | bytes 3145728 | tf_op jit(solution)/shard_map/psum | solution.py:230
  1323.4 96.3 %all-gather.39.cloned.1.call-start = ((), (), s32[]{:S(2)}) async-start(), calls=%async_computation.27 | async-start | bytes 21528576 | tf_op jit(solution)/shard_map/all_gather | solution.py:72
  1327.5 4.2 copy-start.79
  1327.5 4.2 copy-start.80
  1327.6 4.2 copy-start.59
  1327.9 3.9 copy-start.88
  1327.9 4.1 copy-start.54
  1327.9 4.1 copy-start.55
  1327.9 4.2 copy-start.58
  1391.3 39.6 %copy-start.11 = (bf16[1,577,1024]{2,1,0:T(8,128)(2,1)S(1)}, bf16[1,577,1024]{2,1,0:T(8,128)(2,1)}, u32[]{:S(2)}) copy-start(bf16[1,577,1024]{2,1,0:T(8,128)(2,1)} %param.14) | copy-start | bytes 3545092
  1436.2 3.9 copy-start.56
  1436.3 3.9 copy-start.57
  (46 other events, 93.9 us)
Sparse Core Ops, SparseCore 0:
  92.4 67.1 all-reduce.7
  193.5 65.6 all-reduce.9
  286.6 63.3 all-reduce.11
  386.4 92.9 all-gather.32
  481.8 67.3 all-reduce.13
  589.1 94.2 all-gather.34
  707.0 95.5 all-gather.36
  1326.0 93.6 all-gather.38
Sparse Core Ops, SparseCore 1:
  95.9 46.6 all-gather.24
  145.5 44.1 all-gather.26
  290.1 42.8 all-gather.28
  335.4 44.1 all-gather.30
  712.0 76.5 reduce-scatter.18
  792.2 74.2 reduce-scatter.22
  870.5 69.3 reduce-scatter.14
  943.8 72.7 reduce-scatter.10
  1020.7 74.3 reduce-scatter.16
  1098.9 74.2 reduce-scatter.20
  1177.1 69.2 reduce-scatter.12
  1250.5 72.7 reduce-scatter.8
  1326.2 58.0 all-reduce.15
